TPU v7x, 128 devices: a whole 4x4x4 slice. The times are simulated.
128 devices in a mesh: row: 8 (over z, y_lo), col: 16 (over y_hi, x, core).
Axes of the slice: x: 4, y: 4 (y_hi: 2, y_lo: 2; y = y_hi * 2 + y_lo), z: 4, core: 2. Of those that a mesh axis runs over, the one named last changes fastest.
Arguments:
- subspace: bfloat16 [1024, 12288], P('col', 'row')
- rotation: bfloat16 [1024, 1024], replicated, may hold values from -0.1875 to 0.1875
- block_tiles: bfloat16 [64, 31, 192, 192], P('row'), as said below
- block_cols: int32 [64, 31], P('row'), may hold values from 0 to 63, as said below
Outputs:
- filtered: bfloat16 [1024, 12288], P('col', 'row')
- gram_matrix: float32 [1024, 1024], P('col', 'row')
- rayleigh: float32 [1024, 1024], P('col', 'row')
Inputs may be any that keep to these rules, and one draw needn't show every extreme that they name: block_cols[i, 0] = i; for t < 15, block_cols[i, 2t+1] = p_t(i) and block_cols[i, 2t+2] is the inverse of p_t at i, where each p_t is a permutation of the 64 block rows. The stored matrix is symmetric: block_tiles[i, 0] is symmetric and block_tiles[i, 2t+2] is the transpose of block_tiles[j, 2t+1] for the block row j with block_cols[j, 2t+1] = i.
All inputs are finite; a program needn't handle non-finite values.
Results may differ from a plain program's by a relative error of at most 0.014.
Values may be sent and summed in bfloat16 or wider, within the bound.
A program may use at most 128 MiB of HBM per device.

v0:
```python
import functools

import jax
import jax.numpy as jnp
from jax import lax
from jax.experimental import pallas as pl
from jax.experimental.pallas import tpu as pltpu
from jax.sharding import PartitionSpec as P

MESH = pl.DeviceIdType.MESH
DEGREE = 4
CENTER = 1.6
WIDTH = 0.9
ROWS = 8
COLS = 16
BLK = 192
SLOTS = 31
PAIRS = 4
HALF = PAIRS * BLK
PIECE = HALF // COLS
GROUP = 2
LAG = 3
LANES = 128


def swap_halves(values):
    return pltpu.roll(values, LANES // 2, 1)


def kernel(
    cols, sub, rot_hbm, tiles_hbm, filt, gram, ray,
    field0, field1, tiles, rot, packed, raw, mixed, peer, every, terms, parts,
    load_sem, rot_sem, out1, in1, out2, in2, row_out, row_in,
    sib_out, sib_in, col_out, col_in, sum_out, sum_in,
):
    r = lax.axis_index("row")
    c = lax.axis_index("col")
    core = lax.rem(c, 2)
    chip = c // 2
    sibling = c + 1 - 2 * core
    f32, bf16 = jnp.float32, jnp.bfloat16
    fields = (field0, field1)
    lane = lax.broadcasted_iota(jnp.int32, (1, LANES), 1) // (LANES // 2)

    loads = [pltpu.make_async_copy(tiles_hbm.at[i], tiles.at[i], load_sem.at[i]) for i in range(8)]
    rot_load = pltpu.make_async_copy(rot_hbm, rot, rot_sem)
    rot_load.start()
    for load in loads:
        load.start()

    def send(src, dst, out_sem, in_sem, to_row, to_col):
        copy = pltpu.make_async_remote_copy(
            src_ref=src, dst_ref=dst, send_sem=out_sem, recv_sem=in_sem,
            device_id=(to_row, to_col), device_id_type=MESH,
        )
        return copy

    barrier = pltpu.get_barrier_semaphore()
    for d in range(1, COLS):
        pl.semaphore_signal(barrier, inc=1, device_id=(r, lax.rem(c + d, COLS)), device_id_type=MESH)
    for d in range(1, ROWS):
        for k in (0, 1):
            pl.semaphore_signal(
                barrier, inc=1, device_id=(lax.rem(r + d, ROWS), 2 * chip + k), device_id_type=MESH
            )

    natural = jnp.concatenate([sub[:, :HALF], sub[:, HALF:]], axis=0).astype(f32)
    packed[...] = natural.T.astype(bf16)
    for q in range(PAIRS):
        field1[PAIRS * r + q] = jnp.zeros((BLK, LANES), bf16)
    pl.semaphore_wait(barrier, COLS - 1 + 2 * (ROWS - 1))

    sends = []
    for d in range(1, COLS):
        to = lax.rem(c + d, COLS)
        copy = send(
            packed.at[pl.ds(pl.multiple_of(to * PIECE, PIECE), PIECE)], raw.at[c],
            out1.at[d], in1.at[c], r, to,
        )
        copy.start()
        sends.append(copy)
    raw[c] = packed[pl.ds(pl.multiple_of(c * PIECE, PIECE), PIECE), :]
    for d in range(1, COLS):
        src = lax.rem(c + d, COLS)
        send(packed.at[pl.ds(0, PIECE)], raw.at[src], out1.at[d], in1.at[src], r, src).wait_recv()
    rot_load.wait()
    left, right = [], []
    for e in range(COLS // 2):
        a, b = raw[2 * e].astype(f32), raw[2 * e + 1].astype(f32)
        left.append(jnp.where(lane == 0, a, swap_halves(b)))
        right.append(jnp.where(lane == 0, swap_halves(a), b))
    wide = jnp.concatenate(
        [jnp.concatenate(left, axis=1), jnp.concatenate(right, axis=1)], axis=0
    ).astype(bf16)
    rotated = jnp.dot(wide, rot[...], preferred_element_type=f32)
    for e in range(COLS // 2):
        a = rotated[:PIECE, e * LANES : (e + 1) * LANES]
        b = rotated[PIECE:, e * LANES : (e + 1) * LANES]
        mixed[2 * e] = jnp.where(lane == 0, a, swap_halves(b)).astype(bf16)
        mixed[2 * e + 1] = jnp.where(lane == 0, swap_halves(a), b).astype(bf16)

    def piece(of):
        return PAIRS * r + of // PAIRS, pl.ds(pl.multiple_of(lax.rem(of, PAIRS) * PIECE, PIECE), PIECE)

    for d in range(1, COLS):
        to = lax.rem(c + d, COLS)
        copy = send(mixed.at[to], field0.at[*piece(c)], out2.at[d], in2.at[c], r, to)
        copy.start()
        sends.append(copy)
    field0[*piece(c)] = mixed[c]
    for d in range(1, COLS):
        src = lax.rem(c + d, COLS)
        send(mixed.at[0], field0.at[*piece(src)], out2.at[d], in2.at[src], r, src).wait_recv()
    for copy in sends:
        copy.wait_send()

    def chunk_rows(q):
        return pl.ds(pl.multiple_of(q * BLK, BLK), BLK)

    z, y = r // 2, lax.rem(r, 2)

    def at(dz, dy):
        return 2 * lax.rem(z + dz + 4, 4) + (lax.rem(y + dy, 2))

    whole_pair, low, high = (0, BLK), (0, BLK // 2), (BLK // 2, BLK // 2)
    by_z, by_y = (0, 128), (128, 64)
    FIRST = (
        ((0, 0), (1, 0), whole_pair),
        ((0, 0), (-1, 0), whole_pair),
        ((0, 0), (0, 1), whole_pair),
    )
    ONWARD = (
        (0, (-1, 0), (1, 0), low),
        (1, (1, 0), (-1, 0), high),
        (0, (-1, 0), (1, 1), low),
        (1, (1, 0), (-1, 1), high),
        (0, (-1, 0), (0, 1), by_y),
        (1, (1, 0), (0, 1), by_y),
        (2, (0, 1), (1, 0), by_z),
        (2, (0, 1), (-1, 0), by_z),
    )

    def row_copy(par, q, n, src, to, part):
        view = fields[par].at[PAIRS * at(*src) + q, pl.ds(part[0], part[1])]
        return send(view, view, row_out.at[q, n], row_in.at[par, q, n], at(*to), c)

    def arrival(par, q, n, src, to, part):
        return row_copy(par, q, n, (src[0] - to[0], src[1] + to[1]), to, part)

    def spread(par, q):
        for n, (src, to, part) in enumerate(FIRST):
            row_copy(par, q, n, src, to, part).start()

    def onward(par, q):
        for n, (src, to, part) in enumerate(FIRST):
            arrival(par, q, n, src, to, part).wait_recv()
            for m, (after, src2, to2, part2) in enumerate(ONWARD):
                if after == n:
                    row_copy(par, q, 3 + m, src2, to2, part2).start()

    def await_all(par):
        def step(q, carry):
            for n, (src, to, part) in enumerate(FIRST):
                row_copy(par, q, n, src, to, part).wait_send()
            for m, (_, src, to, part) in enumerate(ONWARD):
                arrival(par, q, 3 + m, src, to, part).wait_recv()
                row_copy(par, q, 3 + m, src, to, part).wait_send()
            return carry

        lax.fori_loop(0, PAIRS, step, 0)

    def picked(par, i, s):
        col = cols[i, s]
        part = fields[par][((col >> 3) << 2) + (col & 3)]
        return jnp.where(lane == ((col >> 2) & 1), part, jnp.zeros_like(part))

    def applied(par, q):
        totals = [jnp.zeros((BLK, LANES), f32)] * 2
        for s in range(0, SLOTS, GROUP):
            slots = range(s, min(s + GROUP, SLOTS))
            for n in range(2):
                i = q + PAIRS * n
                wide_tiles = jnp.concatenate([tiles[i, t] for t in slots], axis=1)
                blocks = jnp.concatenate([picked(par, i, t) for t in slots], axis=0)
                totals[n] += jnp.dot(wide_tiles, blocks, preferred_element_type=f32)
        first, second = totals
        return jnp.where(lane == 0, first + swap_halves(first), second + swap_halves(second))

    def next_level(par, q, scale):
        now = fields[par][PAIRS * r + q].astype(f32)
        before = fields[1 - par][PAIRS * r + q].astype(f32)
        level = scale * (applied(par, q) - CENTER * now) - before
        fields[1 - par][PAIRS * r + q] = level.astype(bf16)

    for q in range(PAIRS):
        spread(0, q)
    for q in range(PAIRS):
        onward(0, q)
    for load in loads:
        load.wait()

    def sib_copy(which, q):
        src = fields[which].at[PAIRS * r + q]
        return send(
            src, peer.at[which, q], sib_out.at[which, q], sib_in.at[which, q], r, sibling
        )

    def merged_pair(which, q):
        own = fields[which][PAIRS * r + q].astype(f32)
        other = swap_halves(peer[which, q].astype(f32))
        return jnp.where(lane == core, own, other)

    high_y, x = chip // 4, lax.rem(chip, 4)
    ACROSS = ((1, 0), (3, 0), (2, 0))
    COL = ((0, 1), *ACROSS)

    def chip_at(dx, dy):
        return 4 * lax.rem(high_y + dy, 2) + lax.rem(x + dx, 4)

    def col_copy(q, n, source_chip, to):
        view = every.at[source_chip, q]
        return send(view, view, col_out.at[q, n], col_in.at[q, n], r, 2 * to + core)

    def col_first(q):
        sib_copy(0, q).wait()
        every[chip, q] = merged_pair(0, q).astype(bf16)
        for n, to in enumerate(COL):
            col_copy(q, n, chip, chip_at(*to)).start()

    def col_onward(q):
        other = chip_at(0, 1)
        col_copy(q, 0, other, other).wait_recv()
        for n, to in enumerate(ACROSS):
            col_copy(q, 4 + n, other, chip_at(*to)).start()

    def col_await():
        def step(q, carry):
            other = chip_at(0, 1)
            col_copy(q, 0, chip, other).wait_send()
            for n, to in enumerate(ACROSS):
                col_copy(q, 1 + n, chip, chip_at(*to)).wait_send()
                col_copy(q, 4 + n, other, chip_at(*to)).wait_send()
                col_copy(q, 1 + n, chip_at(4 - to[0], 0), chip_at(*to)).wait_recv()
                col_copy(q, 4 + n, chip_at(4 - to[0], 1), chip_at(*to)).wait_recv()
            return carry

        lax.fori_loop(0, PAIRS, step, 0)

    def one_level(par, scale, last):
        await_all(par)

        def pair(q, carry):
            next_level(par, q, scale)
            spread(1 - par, q)
            if last is not None:

                @pl.when(last)
                def _():
                    sib_copy(0, q).start()

                    @pl.when(q >= 1)
                    def _():
                        col_first(q - 1)

            @pl.when(q >= LAG)
            def _():
                onward(1 - par, q - LAG)

            return carry

        lax.fori_loop(0, PAIRS, pair, 0)
        if last is not None:

            @pl.when(last)
            def _():
                col_first(PAIRS - 1)

        for q in range(PAIRS - LAG, PAIRS):
            onward(1 - par, q)

    def two_levels(k, carry):
        one_level(0, jnp.where(k == 0, 1.0 / WIDTH, 2.0 / WIDTH), None)
        one_level(1, 2.0 / WIDTH, k == DEGREE // 2 - 1)
        return carry

    lax.fori_loop(0, DEGREE // 2, two_levels, 0)

    lax.fori_loop(0, PAIRS, lambda q, carry: (col_onward(q), carry)[1], 0)
    flat = jnp.concatenate([field0[PAIRS * r + q] for q in range(PAIRS)], axis=0)
    flat = flat.astype(f32).T.astype(bf16)
    filt[:, :HALF] = flat[: LANES // 2]
    filt[:, HALF:] = flat[LANES // 2 :]
    own_half = every[chip].reshape(HALF, LANES).astype(f32).T.astype(bf16)
    await_all(0)

    source = 2 * r + core

    def sum_copy(w, n, to_row, to_core, src):
        return send(
            terms.at[w, to_row, to_core], parts.at[w, src], sum_out.at[w, n], sum_in.at[w, src],
            to_row, 2 * chip + to_core,
        )

    def member(n):
        index = lax.rem(source + n, 2 * ROWS)
        return index // 2, lax.rem(index, 2), index

    def send_terms(w, modes):
        for e in range(ROWS):
            product = jnp.dot(
                modes, every[e].reshape(HALF, LANES), preferred_element_type=f32
            ).astype(bf16)
            terms[w, e, 0] = product[: LANES // 2]
            terms[w, e, 1] = product[LANES // 2 :]
        for n in range(1, 2 * ROWS):
            to_row, to_core, _ = member(n)
            sum_copy(w, n, to_row, to_core, source).start()
        parts[w, source] = terms[w, r, core]

    def add_terms(w):
        for n in range(1, 2 * ROWS):
            to_row, to_core, index = member(n)
            sum_copy(w, n, r, core, index).wait_recv()
            sum_copy(w, n, to_row, to_core, source).wait_send()
        total = parts[w, 0].astype(f32)
        for n in range(1, 2 * ROWS):
            total += parts[w, n].astype(f32)
        return total * (1.0 / (ROWS * 2 * HALF))

    def image_pair(q):
        field1[PAIRS * r + q] = applied(0, q).astype(bf16)
        sib_copy(1, q).start()

    def image_step(q, carry):
        image_pair(q)

        @pl.when(q == PAIRS - 2)
        def _():
            col_await()
            send_terms(0, own_half)

        return carry

    lax.fori_loop(0, PAIRS, image_step, 0)
    halves = []
    for q in range(PAIRS):
        sib_copy(1, q).wait()
        halves.append(merged_pair(1, q))
    send_terms(1, jnp.concatenate(halves, axis=0).T.astype(bf16))
    gram[...] = add_terms(0)
    ray[...] = add_terms(1)


def copy_out(filt, gram, ray, filt_out, gram_out, ray_out):
    filt_out[...] = filt[...]
    gram_out[...] = gram[...]
    ray_out[...] = ray[...]


def local(subspace, rotation, block_tiles, block_cols):
    bf16, f32 = jnp.bfloat16, jnp.float32
    vmem = pl.BlockSpec(memory_space=pltpu.VMEM)
    dma = pltpu.SemaphoreType.DMA
    results = pl.pallas_call(
        kernel,
        out_shape=(
            jax.ShapeDtypeStruct(subspace.shape, bf16),
            jax.ShapeDtypeStruct((LANES // 2, LANES), f32),
            jax.ShapeDtypeStruct((LANES // 2, LANES), f32),
        ),
        in_specs=[
            pl.BlockSpec(memory_space=pltpu.SMEM),
            vmem,
            pl.BlockSpec(memory_space=pl.ANY),
            pl.BlockSpec(memory_space=pl.ANY),
        ],
        out_specs=(vmem, vmem, vmem),
        scratch_shapes=[
            pltpu.VMEM((ROWS * PAIRS, BLK, LANES), bf16),
            pltpu.VMEM((ROWS * PAIRS, BLK, LANES), bf16),
            pltpu.VMEM(block_tiles.shape, bf16),
            pltpu.VMEM(rotation.shape, bf16),
            pltpu.VMEM((HALF, LANES), bf16),
            pltpu.VMEM((COLS, PIECE, LANES), bf16),
            pltpu.VMEM((COLS, PIECE, LANES), bf16),
            pltpu.VMEM((2, PAIRS, BLK, LANES), bf16),
            pltpu.VMEM((ROWS, PAIRS, BLK, LANES), bf16),
            pltpu.VMEM((2, ROWS, 2, LANES // 2, LANES), bf16),
            pltpu.VMEM((2, 2 * ROWS, LANES // 2, LANES), bf16),
            dma((8,)),
            dma,
            dma((COLS,)),
            dma((COLS,)),
            dma((COLS,)),
            dma((COLS,)),
            dma((PAIRS, 11)),
            dma((2, PAIRS, 11)),
            dma((2, PAIRS)),
            dma((2, PAIRS)),
            dma((PAIRS, 7)),
            dma((PAIRS, 7)),
            dma((2, 2 * ROWS)),
            dma((2, 2 * ROWS)),
        ],
        compiler_params=pltpu.CompilerParams(
            collective_id=0, has_side_effects=True, vmem_limit_bytes=56 * 2**20
        ),
        cost_estimate=pl.CostEstimate(flops=7_000_000_000, bytes_accessed=30_000_000, transcendentals=0),
    )(block_cols, subspace, rotation, block_tiles)
    return pl.pallas_call(
        copy_out,
        out_shape=tuple(jax.ShapeDtypeStruct(x.shape, x.dtype) for x in results),
        in_specs=[vmem] * 3,
        out_specs=(vmem,) * 3,
    )(*results)


def solution(mesh):
    return jax.shard_map(
        local,
        mesh=mesh,
        in_specs=(P("col", "row"), P(), P("row", None, None, None), P("row", None)),
        out_specs=(P("col", "row"), P("col", "row"), P("col", "row")),
        check_vma=False,
    )
```

profile of v0, /device:TPU:1, one launch (start us, length us, event | category | flops | bytes accessed | tf_op | source)
XLA Modules:
  0.0 123.9 jit_solution(10700816481004864989)
XLA Ops:
  0.6 121.6 %shard_map.67 = (bf16[64,1536]{1,0:T(8,128)(2,1)}, f32[64,128]{1,0:T(8,128)}, f32[64,128]{1,0:T(8,128)}) custom-call(s32[8,31]{1,0:T(8,128)} %cols.1, bf16[64,1536]{1,0:T(8,128)(2,1)} %sub.1, bf16[1024,1024]{1,0:T(8,128)(2,1)} %rot_hbm.1, bf16[8,31,192,192]{3,2,1,0:T(8,128)(2,1)} %tiles_hbm.1), custom_call_target="tpu_custom_call" | custom-call | flops 7000000000 | bytes 30000000 | tf_op jit(solution)/shard_map/pallas_call | solution.py:364
  122.3 1.6 %shard_map.68 = (bf16[64,1536]{1,0:T(8,128)(2,1)}, f32[64,128]{1,0:T(8,128)}, f32[64,128]{1,0:T(8,128)}) custom-call(bf16[64,1536]{1,0:T(8,128)(2,1)} %get-tuple-element.6.filt, f32[64,128]{1,0:T(8,128)} %get-tuple-element.7.gram, f32[64,128]{1,0:T(8,128)} %get-tuple-element.8.ray), custom_call_target="tpu_custom_call" | custom-call | tf_op jit(solution)/shard_map/pallas_call | solution.py:410
where the time goes:
time: 124 us
  Pallas kernels  123 us (99%)
    pallas_call x1, Pallas kernels, local(): pl.pallas_call(kernel, out_shape=(jax.ShapeDtypeStruct(subspace.shape, bf...  122 us

commit v1 on v0

--- a/solution.py
+++ b/solution.py
@@ -19,7 +19,7 @@
 HALF = PAIRS * BLK
 PIECE = HALF // COLS
 GROUP = 2
-LAG = 3
+THREE_LEGS = 2
 LANES = 128
 
 
@@ -123,22 +123,27 @@
         return 2 * lax.rem(z + dz + 4, 4) + (lax.rem(y + dy, 2))
 
     whole_pair, low, high = (0, BLK), (0, BLK // 2), (BLK // 2, BLK // 2)
-    by_z, by_y = (0, 128), (128, 64)
     FIRST = (
         ((0, 0), (1, 0), whole_pair),
         ((0, 0), (-1, 0), whole_pair),
         ((0, 0), (0, 1), whole_pair),
     )
-    ONWARD = (
-        (0, (-1, 0), (1, 0), low),
-        (1, (1, 0), (-1, 0), high),
-        (0, (-1, 0), (1, 1), low),
-        (1, (1, 0), (-1, 1), high),
-        (0, (-1, 0), (0, 1), by_y),
-        (1, (1, 0), (0, 1), by_y),
-        (2, (0, 1), (1, 0), by_z),
-        (2, (0, 1), (-1, 0), by_z),
-    )
+
+    def onward_plan(q):
+        split = 160 if q < THREE_LEGS else 128
+        by_z, by_y = (0, split), (split, BLK - split)
+        plan = (
+            (0, (-1, 0), (1, 0), low),
+            (1, (1, 0), (-1, 0), high),
+            (0, (-1, 0), (0, 1), by_y),
+            (1, (1, 0), (0, 1), by_y),
+            (2, (0, 1), (1, 0), by_z),
+            (2, (0, 1), (-1, 0), by_z),
+        )
+        far = ((0, (-1, 0), (1, 1), low), (1, (1, 0), (-1, 1), high))
+        return plan, far
+
+    THIRD = (((2, 0), (0, 1), low), ((2, 0), (0, 1), high))
 
     def row_copy(par, q, n, src, to, part):
         view = fields[par].at[PAIRS * at(*src) + q, pl.ds(part[0], part[1])]
@@ -152,22 +157,35 @@
             row_copy(par, q, n, src, to, part).start()
 
     def onward(par, q):
+        plan, far = onward_plan(q)
+        steps = plan if q < THREE_LEGS else plan + far
         for n, (src, to, part) in enumerate(FIRST):
             arrival(par, q, n, src, to, part).wait_recv()
-            for m, (after, src2, to2, part2) in enumerate(ONWARD):
+            for m, (after, src2, to2, part2) in enumerate(steps):
                 if after == n:
                     row_copy(par, q, 3 + m, src2, to2, part2).start()
 
+    def third(par, q):
+        plan, _ = onward_plan(q)
+        for m in range(2):
+            arrival(par, q, 3 + m, *plan[m][1:]).wait_recv()
+            row_copy(par, q, 9 + m, *THIRD[m]).start()
+
     def await_all(par):
-        def step(q, carry):
+        for q in range(PAIRS):
+            plan, far = onward_plan(q)
+            if q < THREE_LEGS:
+                last = tuple((0, *step) for step in THIRD)
+                pending = plan[2:] + last
+            else:
+                last = far
+                pending = plan + last
             for n, (src, to, part) in enumerate(FIRST):
                 row_copy(par, q, n, src, to, part).wait_send()
-            for m, (_, src, to, part) in enumerate(ONWARD):
-                arrival(par, q, 3 + m, src, to, part).wait_recv()
+            for m, (_, src, to, part) in enumerate(plan + last):
+                if (_, src, to, part) in pending:
+                    arrival(par, q, 3 + m, src, to, part).wait_recv()
                 row_copy(par, q, 3 + m, src, to, part).wait_send()
-            return carry
-
-        lax.fori_loop(0, PAIRS, step, 0)
 
     def picked(par, i, s):
         col = cols[i, s]
@@ -196,6 +214,8 @@
         spread(0, q)
     for q in range(PAIRS):
         onward(0, q)
+    for q in range(THREE_LEGS):
+        third(0, q)
     for load in loads:
         load.wait()
 
@@ -262,10 +282,6 @@
                     def _():
                         col_first(q - 1)
 
-            @pl.when(q >= LAG)
-            def _():
-                onward(1 - par, q - LAG)
-
             return carry
 
         lax.fori_loop(0, PAIRS, pair, 0)
@@ -275,8 +291,10 @@
             def _():
                 col_first(PAIRS - 1)
 
-        for q in range(PAIRS - LAG, PAIRS):
+        for q in range(PAIRS):
             onward(1 - par, q)
+        for q in range(THREE_LEGS):
+            third(1 - par, q)
 
     def two_levels(k, carry):
         one_level(0, jnp.where(k == 0, 1.0 / WIDTH, 2.0 / WIDTH), None)

time: 124 us -> 120 us (0.968)
  Pallas kernels: 123 us -> 119 us
    pallas_call x1, Pallas kernels: 122 us -> 118 us  [local(): pl.pallas_call(kernel, out_shape=(jax.ShapeDtypeStruct(subspace.shape, bf...]
where the time goes in v1:
time: 120 us
  Pallas kernels  119 us (99%)
    pallas_call x1, Pallas kernels, local(): pl.pallas_call(kernel, out_shape=(jax.ShapeDtypeStruct(subspace.shape, bf...  118 us

profile of v1, /device:TPU:1, one launch (start us, length us, event | category | flops | bytes accessed | tf_op | source)
XLA Modules:
  0.0 120.1 jit_solution(11956977984013431541)
XLA Ops:
  0.6 117.8 %shard_map.67 = (bf16[64,1536]{1,0:T(8,128)(2,1)}, f32[64,128]{1,0:T(8,128)}, f32[64,128]{1,0:T(8,128)}) custom-call(s32[8,31]{1,0:T(8,128)} %cols.1, bf16[64,1536]{1,0:T(8,128)(2,1)} %sub.1, bf16[1024,1024]{1,0:T(8,128)(2,1)} %rot_hbm.1, bf16[8,31,192,192]{3,2,1,0:T(8,128)(2,1)} %tiles_hbm.1), custom_call_target="tpu_custom_call" | custom-call | flops 7000000000 | bytes 30000000 | tf_op jit(solution)/shard_map/pallas_call | solution.py:382
  118.4 1.6 %shard_map.68 = (bf16[64,1536]{1,0:T(8,128)(2,1)}, f32[64,128]{1,0:T(8,128)}, f32[64,128]{1,0:T(8,128)}) custom-call(bf16[64,1536]{1,0:T(8,128)(2,1)} %get-tuple-element.6.filt, f32[64,128]{1,0:T(8,128)} %get-tuple-element.7.gram, f32[64,128]{1,0:T(8,128)} %get-tuple-element.8.ray), custom_call_target="tpu_custom_call" | custom-call | tf_op jit(solution)/shard_map/pallas_call | solution.py:428

commit v2 on v1

--- a/solution.py
+++ b/solution.py
@@ -55,6 +55,16 @@
         )
         return copy
 
+    far_steps = [
+        (dy, dx, dk) for dy, dx in ((1, 2), (1, 1), (1, 3), (1, 0), (0, 2), (0, 1), (0, 3), (0, 0))
+        for dk in (0, 1)
+    ]
+    far_steps.remove((0, 0, 0))
+
+    def col_peer(d):
+        dy, dx, dk = far_steps[d - 1]
+        return 8 * lax.rem(c // 8 + dy, 2) + 2 * lax.rem(chip + dx, 4) + lax.rem(core + dk, 2)
+
     barrier = pltpu.get_barrier_semaphore()
     for d in range(1, COLS):
         pl.semaphore_signal(barrier, inc=1, device_id=(r, lax.rem(c + d, COLS)), device_id_type=MESH)
@@ -72,7 +82,7 @@
 
     sends = []
     for d in range(1, COLS):
-        to = lax.rem(c + d, COLS)
+        to = col_peer(d)
         copy = send(
             packed.at[pl.ds(pl.multiple_of(to * PIECE, PIECE), PIECE)], raw.at[c],
             out1.at[d], in1.at[c], r, to,
@@ -81,7 +91,7 @@
         sends.append(copy)
     raw[c] = packed[pl.ds(pl.multiple_of(c * PIECE, PIECE), PIECE), :]
     for d in range(1, COLS):
-        src = lax.rem(c + d, COLS)
+        src = col_peer(COLS - d)
         send(packed.at[pl.ds(0, PIECE)], raw.at[src], out1.at[d], in1.at[src], r, src).wait_recv()
     rot_load.wait()
     left, right = [], []
@@ -103,13 +113,13 @@
         return PAIRS * r + of // PAIRS, pl.ds(pl.multiple_of(lax.rem(of, PAIRS) * PIECE, PIECE), PIECE)
 
     for d in range(1, COLS):
-        to = lax.rem(c + d, COLS)
+        to = col_peer(d)
         copy = send(mixed.at[to], field0.at[*piece(c)], out2.at[d], in2.at[c], r, to)
         copy.start()
         sends.append(copy)
     field0[*piece(c)] = mixed[c]
     for d in range(1, COLS):
-        src = lax.rem(c + d, COLS)
+        src = col_peer(COLS - d)
         send(mixed.at[0], field0.at[*piece(src)], out2.at[d], in2.at[src], r, src).wait_recv()
     for copy in sends:
         copy.wait_send()
@@ -319,9 +329,16 @@
             to_row, 2 * chip + to_core,
         )
 
+    row_steps = [
+        (dz, dy, dk) for dz, dy in ((2, 1), (1, 1), (-1, 1), (2, 0), (1, 0), (-1, 0), (0, 1), (0, 0))
+        for dk in (0, 1)
+    ]
+    row_steps.remove((0, 0, 0))
+
     def member(n):
-        index = lax.rem(source + n, 2 * ROWS)
-        return index // 2, lax.rem(index, 2), index
+        dz, dy, dk = row_steps[n - 1]
+        to_row, to_core = at(dz, dy), lax.rem(core + dk, 2)
+        return to_row, to_core, 2 * to_row + to_core
 
     def send_terms(w, modes):
         for e in range(ROWS):

time: 120 us -> 119 us (level)
  no operation moved by 1% of the time
where the time goes in v2:
time: 119 us
  Pallas kernels  118 us (99%)
    pallas_call x1, Pallas kernels, local(): pl.pallas_call(kernel, out_shape=(jax.ShapeDtypeStruct(subspace.shape, bf...  117 us

profile of v2, /device:TPU:1, one launch (start us, length us, event | category | flops | bytes accessed | tf_op | source)
XLA Modules:
  0.0 119.0 jit_solution(13665259336619455626)
XLA Ops:
  0.6 116.7 %shard_map.67 = (bf16[64,1536]{1,0:T(8,128)(2,1)}, f32[64,128]{1,0:T(8,128)}, f32[64,128]{1,0:T(8,128)}) custom-call(s32[8,31]{1,0:T(8,128)} %cols.1, bf16[64,1536]{1,0:T(8,128)(2,1)} %sub.1, bf16[1024,1024]{1,0:T(8,128)(2,1)} %rot_hbm.1, bf16[8,31,192,192]{3,2,1,0:T(8,128)(2,1)} %tiles_hbm.1), custom_call_target="tpu_custom_call" | custom-call | flops 7000000000 | bytes 30000000 | tf_op jit(solution)/shard_map/pallas_call | solution.py:399
  117.3 1.6 %shard_map.68 = (bf16[64,1536]{1,0:T(8,128)(2,1)}, f32[64,128]{1,0:T(8,128)}, f32[64,128]{1,0:T(8,128)}) custom-call(bf16[64,1536]{1,0:T(8,128)(2,1)} %get-tuple-element.6.filt, f32[64,128]{1,0:T(8,128)} %get-tuple-element.7.gram, f32[64,128]{1,0:T(8,128)} %get-tuple-element.8.ray), custom_call_target="tpu_custom_call" | custom-call | tf_op jit(solution)/shard_map/pallas_call | solution.py:445

commit v3 on v2

--- a/solution.py
+++ b/solution.py
@@ -29,7 +29,7 @@
 
 def kernel(
     cols, sub, rot_hbm, tiles_hbm, filt, gram, ray,
-    field0, field1, tiles, rot, packed, raw, mixed, peer, every, terms, parts,
+    field0, field1, tiles, rot, packed, raw, mixed, peer, every, sums, terms, parts,
     load_sem, rot_sem, out1, in1, out2, in2, row_out, row_in,
     sib_out, sib_in, col_out, col_in, sum_out, sum_in,
 ):
@@ -340,11 +340,9 @@
         to_row, to_core = at(dz, dy), lax.rem(core + dk, 2)
         return to_row, to_core, 2 * to_row + to_core
 
-    def send_terms(w, modes):
+    def send_terms(w, product_with):
         for e in range(ROWS):
-            product = jnp.dot(
-                modes, every[e].reshape(HALF, LANES), preferred_element_type=f32
-            ).astype(bf16)
+            product = product_with(e).astype(bf16)
             terms[w, e, 0] = product[: LANES // 2]
             terms[w, e, 1] = product[LANES // 2 :]
         for n in range(1, 2 * ROWS):
@@ -372,16 +370,29 @@
         @pl.when(q == PAIRS - 2)
         def _():
             col_await()
-            send_terms(0, own_half)
+            send_terms(
+                0,
+                lambda e: jnp.dot(
+                    own_half, every[e].reshape(HALF, LANES), preferred_element_type=f32
+                ),
+            )
 
         return carry
 
     lax.fori_loop(0, PAIRS, image_step, 0)
     halves = []
-    for q in range(PAIRS):
+    for q in range(PAIRS - 1):
         sib_copy(1, q).wait()
         halves.append(merged_pair(1, q))
-    send_terms(1, jnp.concatenate(halves, axis=0).T.astype(bf16))
+    early = jnp.concatenate(halves, axis=0).T.astype(bf16)
+    for e in range(ROWS):
+        blocks = every[e, : PAIRS - 1].reshape(HALF - BLK, LANES)
+        sums[e] = jnp.dot(early, blocks, preferred_element_type=f32)
+    sib_copy(1, PAIRS - 1).wait()
+    late = merged_pair(1, PAIRS - 1).T.astype(bf16)
+    send_terms(
+        1, lambda e: sums[e] + jnp.dot(late, every[e, PAIRS - 1], preferred_element_type=f32)
+    )
     gram[...] = add_terms(0)
     ray[...] = add_terms(1)
 
@@ -420,6 +431,7 @@
             pltpu.VMEM((COLS, PIECE, LANES), bf16),
             pltpu.VMEM((2, PAIRS, BLK, LANES), bf16),
             pltpu.VMEM((ROWS, PAIRS, BLK, LANES), bf16),
+            pltpu.VMEM((ROWS, LANES, LANES), f32),
             pltpu.VMEM((2, ROWS, 2, LANES // 2, LANES), bf16),
             pltpu.VMEM((2, 2 * ROWS, LANES // 2, LANES), bf16),
             dma((8,)),

time: 119 us -> 119 us (level)
  no operation moved by 1% of the time
where the time goes in v3:
time: 119 us
  Pallas kernels  118 us (99%)
    pallas_call x1, Pallas kernels, local(): pl.pallas_call(kernel, out_shape=(jax.ShapeDtypeStruct(subspace.shape, bf...  116 us

profile of v3, /device:TPU:1, one launch (start us, length us, event | category | flops | bytes accessed | tf_op | source)
XLA Modules:
  0.0 118.7 jit_solution(7516099905158435785)
XLA Ops:
  0.6 116.4 %shard_map.67 = (bf16[64,1536]{1,0:T(8,128)(2,1)}, f32[64,128]{1,0:T(8,128)}, f32[64,128]{1,0:T(8,128)}) custom-call(s32[8,31]{1,0:T(8,128)} %cols.1, bf16[64,1536]{1,0:T(8,128)(2,1)} %sub.1, bf16[1024,1024]{1,0:T(8,128)(2,1)} %rot_hbm.1, bf16[8,31,192,192]{3,2,1,0:T(8,128)(2,1)} %tiles_hbm.1), custom_call_target="tpu_custom_call" | custom-call | flops 7000000000 | bytes 30000000 | tf_op jit(solution)/shard_map/pallas_call | solution.py:410
  117.1 1.6 %shard_map.68 = (bf16[64,1536]{1,0:T(8,128)(2,1)}, f32[64,128]{1,0:T(8,128)}, f32[64,128]{1,0:T(8,128)}) custom-call(bf16[64,1536]{1,0:T(8,128)(2,1)} %get-tuple-element.6.filt, f32[64,128]{1,0:T(8,128)} %get-tuple-element.7.gram, f32[64,128]{1,0:T(8,128)} %get-tuple-element.8.ray), custom_call_target="tpu_custom_call" | custom-call | tf_op jit(solution)/shard_map/pallas_call | solution.py:457

commit v4 on v3

--- a/solution.py
+++ b/solution.py
@@ -44,9 +44,6 @@
 
     loads = [pltpu.make_async_copy(tiles_hbm.at[i], tiles.at[i], load_sem.at[i]) for i in range(8)]
     rot_load = pltpu.make_async_copy(rot_hbm, rot, rot_sem)
-    rot_load.start()
-    for load in loads:
-        load.start()
 
     def send(src, dst, out_sem, in_sem, to_row, to_col):
         copy = pltpu.make_async_remote_copy(
@@ -73,6 +70,10 @@
             pl.semaphore_signal(
                 barrier, inc=1, device_id=(lax.rem(r + d, ROWS), 2 * chip + k), device_id_type=MESH
             )
+
+    rot_load.start()
+    for load in loads:
+        load.start()
 
     natural = jnp.concatenate([sub[:, :HALF], sub[:, HALF:]], axis=0).astype(f32)
     packed[...] = natural.T.astype(bf16)

time: 119 us -> 119 us (level)
  no operation moved by 1% of the time
where the time goes in v4:
time: 119 us
  Pallas kernels  118 us (99%)
    pallas_call x1, Pallas kernels, local(): pl.pallas_call(kernel, out_shape=(jax.ShapeDtypeStruct(subspace.shape, bf...  116 us

profile of v4, /device:TPU:1, one launch (start us, length us, event | category | flops | bytes accessed | tf_op | source)
XLA Modules:
  0.0 118.7 jit_solution(17954174513696615973)
XLA Ops:
  0.6 116.4 %shard_map.67 = (bf16[64,1536]{1,0:T(8,128)(2,1)}, f32[64,128]{1,0:T(8,128)}, f32[64,128]{1,0:T(8,128)}) custom-call(s32[8,31]{1,0:T(8,128)} %cols.1, bf16[64,1536]{1,0:T(8,128)(2,1)} %sub.1, bf16[1024,1024]{1,0:T(8,128)(2,1)} %rot_hbm.1, bf16[8,31,192,192]{3,2,1,0:T(8,128)(2,1)} %tiles_hbm.1), custom_call_target="tpu_custom_call" | custom-call | flops 7000000000 | bytes 30000000 | tf_op jit(solution)/shard_map/pallas_call | solution.py:411
  117.0 1.6 %shard_map.68 = (bf16[64,1536]{1,0:T(8,128)(2,1)}, f32[64,128]{1,0:T(8,128)}, f32[64,128]{1,0:T(8,128)}) custom-call(bf16[64,1536]{1,0:T(8,128)(2,1)} %get-tuple-element.6.filt, f32[64,128]{1,0:T(8,128)} %get-tuple-element.7.gram, f32[64,128]{1,0:T(8,128)} %get-tuple-element.8.ray), custom_call_target="tpu_custom_call" | custom-call | tf_op jit(solution)/shard_map/pallas_call | solution.py:458
